TPU v7x, 32 devices: a whole 2x2x4 slice. The times are simulated.
32 devices in a mesh: brow: 4 (over z), bcol: 8 (over y, x, core).
Axes of the slice: x: 2, y: 2, z: 4, core: 2. Of those that a mesh axis runs over, the one named last changes fastest.
Arguments:
- blocks: bfloat16 [4, 8, 40, 256, 256], P('brow', 'bcol'), may hold values from -6 to 6
- pattern_rows: int32 [4, 8, 40], P('brow', 'bcol'), may hold values from 0 to 23
- pattern_cols: int32 [4, 8, 40], P('brow', 'bcol'), may hold values from 0 to 11
- live_count: int32 [4, 8], P('brow', 'bcol'), may hold values from 10 to 40, as said below
- degree_scale: float32 [24576], P(('brow', 'bcol')), may hold values from 0.03125 to 0.125
- eigen_block: float32 [32, 24576], P(None, ('brow', 'bcol')), may hold values from -6 to 6
- direction: float32 [32, 24576], P(None, ('brow', 'bcol')), may hold values from -6 to 6
- cutoff: float32 [1], replicated, may hold values from 0.9 to 1
Outputs:
- eigen_next: float32 [32, 24576], P(None, ('brow', 'bcol'))
- direction_next: float32 [32, 24576], P(None, ('brow', 'bcol'))
- residual: float32 [32, 24576], P(None, ('brow', 'bcol'))
- direction_image: float32 [32, 24576], P(None, ('brow', 'bcol'))
Inputs may be any that keep to these rules, and one draw needn't show every extreme that they name: `live_count`: some owner uses all 40 slots in every draw.
All inputs are finite; a program needn't handle non-finite values.
Results may differ from a plain program's by a relative error of at most 0.033.
Values may be sent and summed in bfloat16 or wider, within the bound.
A program may use at most 64 MiB of HBM per device.

v0:
```python
import functools

import jax
import jax.numpy as jnp
from jax import lax
from jax.experimental import pallas as pl
from jax.experimental.pallas import tpu as pltpu
from jax.sharding import PartitionSpec as P

ITERS = 2
NS_STEPS = 8
MESH = pl.DeviceIdType.MESH
LANES = 128


def halves(value):
    high = value.astype(jnp.bfloat16)
    return high, (value - high.astype(jnp.float32)).astype(jnp.bfloat16)


def split_dot(left, right, right_dim):
    rows = left.shape[0]
    left_high, left_low = halves(left)
    right_high, right_low = halves(right)

    def part(first, second):
        return lax.dot_general(
            first,
            second,
            (((1,), (right_dim,)), ((), ())),
            preferred_element_type=jnp.float32,
        )

    main = part(jnp.concatenate([left_high, left_low], 0), right_high)
    return main[:rows] + (main[rows:] + part(left_high, right_low))


def dot(left, right):
    return split_dot(left, right, 0)


def dot_nt(left, right):
    return split_dot(left, right, 1)


def grid_ids(rows):
    shape = (rows, LANES)
    return (
        lax.broadcasted_iota(jnp.int32, shape, 0),
        lax.broadcasted_iota(jnp.int32, shape, 1),
    )


def pad_rows(value, before=0):
    parts = [value, jnp.zeros((LANES - before - value.shape[0], LANES), jnp.float32)]
    if before:
        parts.insert(0, jnp.zeros((before, LANES), jnp.float32))
    return jnp.concatenate(parts, 0)


def inverse_pair(a, b, d):
    scale = 1.0 / (a * d - b * b)
    return d * scale, -(b * scale), a * scale


def inverse_four(m):
    p, q, r = inverse_pair(m[0][0], m[0][1], m[1][1])
    e = [[p * m[0][2 + c] + q * m[1][2 + c] for c in range(2)],
         [q * m[0][2 + c] + r * m[1][2 + c] for c in range(2)]]

    def schur(i, j):
        return m[2 + i][2 + j] - (m[0][2 + i] * e[0][j] + m[1][2 + i] * e[1][j])

    x, y, z = inverse_pair(schur(0, 0), schur(0, 1), schur(1, 1))
    f = [[e[i][0] * x + e[i][1] * y, e[i][0] * y + e[i][1] * z] for i in range(2)]

    def corner(i, j):
        return f[i][0] * e[j][0] + f[i][1] * e[j][1]

    off = q + corner(0, 1)
    return [
        [p + corner(0, 0), off, -f[0][0], -f[0][1]],
        [off, r + corner(1, 1), -f[1][0], -f[1][1]],
        [-f[0][0], -f[1][0], x, y],
        [-f[0][1], -f[1][1], y, z],
    ]


def inverse(matrix):
    side = matrix.shape[0]
    row_id, col_id = grid_ids(side)
    width = 4
    assert side % width == 0

    def sweep(step, now):
        first = step * width
        at_row = [row_id == first + k for k in range(width)]
        at_col = [col_id == first + k for k in range(width)]
        cols = [
            jnp.sum(jnp.where(at_col[k], now, 0.0), axis=1, keepdims=True)
            for k in range(width)
        ]
        rows = [
            jnp.sum(jnp.where(at_row[k], now, 0.0), axis=0, keepdims=True)
            for k in range(width)
        ]
        wide = [jnp.broadcast_to(col, now.shape) for col in cols]
        pivots = [
            [
                jnp.sum(jnp.where(at_row[i], wide[j], 0.0), axis=0, keepdims=True)
                for j in range(width)
            ]
            for i in range(width)
        ]
        inner = inverse_four(pivots)
        scaled_rows = [
            (inner[i][0] * rows[0] + inner[i][1] * rows[1])
            + (inner[i][2] * rows[2] + inner[i][3] * rows[3])
            for i in range(width)
        ]
        out = now - (
            (wide[0] * scaled_rows[0] + wide[1] * scaled_rows[1])
            + (wide[2] * scaled_rows[2] + wide[3] * scaled_rows[3])
        )
        for i in range(width):
            scaled_col = (wide[0] * inner[0][i] + wide[1] * inner[1][i]) + (
                wide[2] * inner[2][i] + wide[3] * inner[3][i]
            )
            out = jnp.where(at_col[i], scaled_col, out)
        for i in range(width):
            line = scaled_rows[i]
            for j in range(width):
                line = jnp.where(at_col[j][0:1], -inner[i][j], line)
            out = jnp.where(at_row[i], line, out)
        return out

    return -lax.fori_loop(0, side // width, sweep, matrix)


def extend_inverse(known, border, offset):
    side = border.shape[0]
    row_id, col_id = grid_ids(side)
    placed = (col_id == row_id + offset).astype(jnp.float32)
    edge = pad_rows(placed - dot(border, known))
    middle = inverse(dot_nt(border, edge))
    return known + dot(edge.T, pad_rows(dot(middle, edge)))


def body(
    n_row, n_col, piece, slots, wanted,
    tables, cutoff, blocks_hbm, scale_ref, eigen_ref, direction_ref,
    out_x, out_p, out_r, out_ip,
    blocks, basis, image, work, sums,
    gather_x, gather_r, part_x, part_r, land_x, land_r,
    own_x, cols_x, rows_x, all_x, gram_ref, cross_ref,
    block_sem, gx_send, gx_recv, gr_send, gr_recv, px_send, px_recv, pr_send, pr_recv,
    c_send, c_recv, r_send, r_recv, a_send, a_recv,
):
    me_row, me_col = lax.axis_index("brow"), lax.axis_index("bcol")
    side = blocks.shape[-1]
    block_copy = pltpu.make_async_copy(blocks_hbm, blocks, block_sem)
    block_copy.start()

    def row_peer(step):
        return lax.rem(me_row + step, n_row)

    def col_peer(step):
        return lax.rem(me_col + step, n_col)

    barrier = pltpu.get_barrier_semaphore()
    for step in range(1, n_row):
        pl.semaphore_signal(
            barrier, inc=1, device_id=(row_peer(step), me_col), device_id_type=MESH
        )
    for step in range(1, n_col):
        pl.semaphore_signal(
            barrier, inc=1, device_id=(me_row, col_peer(step)), device_id_type=MESH
        )

    scale = scale_ref[...].reshape(1, piece * side)
    basis[0:wanted] = eigen_ref[...]
    basis[wanted : 2 * wanted] = direction_ref[...]
    basis[2 * wanted :] = jnp.zeros((LANES - 2 * wanted, piece * side), jnp.float32)
    image[...] = jnp.zeros(image.shape, jnp.float32)
    sums[slots] = jnp.zeros(sums.shape[1:], jnp.float32)

    pl.semaphore_wait(barrier, n_row + n_col - 2)
    row_id, col_id = grid_ids(LANES)
    eye = jnp.where((row_id == col_id) & (row_id < 3 * wanted), 1.0, 0.0)

    def remote(src, dst, send, recv, device):
        return pltpu.make_async_remote_copy(
            src_ref=src, dst_ref=dst, send_sem=send, recv_sem=recv,
            device_id=device, device_id_type=MESH,
        )

    def spot(p):
        return slice(p * side, (p + 1) * side)

    def apply_graph(turn, first, count, gather, part, land, sems, meanwhile):
        g_send, g_recv, p_send, p_recv = sems
        rows = slice(first, first + count)
        mine = pl.ds(me_row * piece, piece)
        for p in range(piece):
            gather[turn, me_row * piece + p] = (
                scale[:, spot(p)] * basis[rows, spot(p)]
            ).astype(jnp.bfloat16)
        copies = []
        for step in range(1, n_row):
            copies.append(
                remote(
                    gather.at[turn, mine], gather.at[turn, mine],
                    g_send.at[turn, step - 1], g_recv.at[turn, step - 1],
                    (row_peer(step), me_col),
                )
            )
            copies[-1].start()
        found = meanwhile()
        for copy in copies:
            copy.wait()

        def move(k, carry):
            work[k, 0:count] = gather[turn, k]
            return carry

        lax.fori_loop(0, n_row * piece, move, 0)

        def slot(s, carry):
            product = lax.dot_general(
                work[tables[s], 0:count],
                blocks[s],
                (((1,), (1,)), ((), ())),
                preferred_element_type=jnp.float32,
            )
            sums[s, 0:count] = product + sums[tables[slots + s], 0:count]
            return carry

        lax.fori_loop(0, slots, slot, 0, unroll=4)

        def row_sum(owner, p):
            return sums[tables[2 * slots + owner * piece + p], 0:count]

        copies = []
        for step in range(1, n_col):
            owner = col_peer(step)
            for p in range(piece):
                part[turn, step - 1, p] = row_sum(owner, p).astype(jnp.bfloat16)
            copies.append(
                remote(
                    part.at[turn, step - 1], land.at[turn, step - 1],
                    p_send.at[turn, step - 1], p_recv.at[turn, step - 1],
                    (me_row, owner),
                )
            )
            copies[-1].start()
        for copy in copies:
            copy.wait()
        for p in range(piece):
            total = row_sum(me_col, p)
            for step in range(1, n_col):
                total = total + land[turn, step - 1, p].astype(jnp.float32)
            image[rows, spot(p)] = basis[rows, spot(p)] - scale[:, spot(p)] * total
        return found

    def swap(turn, land, send, recv, along_col, source):
        me = me_col if along_col else me_row
        copies = []
        for step in range(1, n_col if along_col else n_row):
            peer = col_peer(step) if along_col else row_peer(step)
            device = (me_row, peer) if along_col else (peer, me_col)
            copies.append(
                remote(
                    source(peer), land.at[turn, me],
                    send.at[turn, step - 1], recv.at[turn, step - 1], device,
                )
            )
            copies[-1].start()
        for copy in copies:
            copy.wait()

    def total_of(land, turn, count):
        value = land[turn, 0]
        for k in range(1, count):
            value = value + land[turn, k]
        return value

    def add_up(turn, value):
        height = LANES // n_col
        for k in range(n_col):
            own_x[turn, k] = value[k * height : (k + 1) * height]
        cols_x[turn, me_col] = own_x[turn, me_col]
        swap(turn, cols_x, c_send, c_recv, True, lambda peer: own_x.at[turn, peer])
        rows_x[turn, me_row] = total_of(cols_x, turn, n_col)
        swap(turn, rows_x, r_send, r_recv, False, lambda peer: rows_x.at[turn, me_row])
        all_x[turn, me_col] = total_of(rows_x, turn, n_row)
        swap(turn, all_x, a_send, a_recv, True, lambda peer: all_x.at[turn, me_col])
        return jnp.concatenate([all_x[turn, k] for k in range(n_col)], 0)

    pair = slice(0, 2 * wanted)
    third = slice(2 * wanted, 3 * wanted)
    x_sems = (gx_send, gx_recv, px_send, px_recv)
    r_sems = (gr_send, gr_recv, pr_send, pr_recv)

    apply_graph(0, 0, 2 * wanted, gather_x, part_x, land_x, x_sems, block_copy.wait)
    both = jnp.concatenate([basis[pair], image[pair]], 0)
    grams = add_up(ITERS, pad_rows(dot_nt(basis[pair], both)))
    gram_ref[...] = jnp.where(col_id < 2 * wanted, grams, 0.0)
    cross_ref[...] = pad_rows(grams.T[2 * wanted :]).T

    def section(turn, carry):
        narrow = grid_ids(wanted)[1] < wanted
        half = grid_ids(wanted)[1] < 2 * wanted
        gram_pair = gram_ref[...]
        cross_pair = cross_ref[...]
        gram_inv = pad_rows(inverse(jnp.where(narrow, gram_pair[0:wanted], 0.0)))
        rayleigh_t = jnp.where(narrow, cross_pair.T[0:wanted], 0.0)
        quotient_t = dot(rayleigh_t, gram_inv)
        basis[third] = image[0:wanted] - dot(quotient_t, basis[...])

        @pl.when(turn < ITERS)
        def _():
            def pair_algebra():
                return extend_inverse(
                    gram_inv, jnp.where(half, gram_pair[wanted : 2 * wanted], 0.0), wanted
                )

            pair_inv = apply_graph(
                turn, 2 * wanted, wanted, gather_r, part_r, land_r, r_sems, pair_algebra
            )
            everything = jnp.concatenate([basis[...], image[...]], 0)
            by_residual = dot_nt(basis[third], everything)
            border = add_up(
                turn,
                pad_rows(
                    jnp.concatenate(
                        [
                            by_residual[:, :LANES],
                            by_residual[:, LANES:],
                            dot_nt(image[third], basis[...]),
                        ],
                        0,
                    )
                ),
            )

            def around(rows, cols):
                low = pad_rows(rows, 2 * wanted)
                right = pad_rows(cols, 2 * wanted).T
                return low + jnp.where(row_id < 2 * wanted, right, 0.0)

            full_inv = extend_inverse(pair_inv, border[0:wanted], 2 * wanted)
            gram_b = gram_pair + around(border[0:wanted], border[0:wanted])
            cross = cross_pair + around(border[wanted : 2 * wanted], border[third])
            gram_a = 0.5 * (cross + cross.T)
            shifted = cutoff[0] * eye - dot(gram_a, full_inv)
            square = dot(shifted, shifted)
            trace = jnp.sum(
                jnp.sum(jnp.where(row_id == col_id, square, 0.0), axis=1, keepdims=True),
                axis=0,
                keepdims=True,
            )
            norm = 1.0 / jnp.sqrt(trace + 1e-06)
            sign = (1.5 * norm) * shifted - (0.5 * norm) * dot(
                shifted * norm, square * norm
            )

            def newton(_, now):
                return 1.5 * now - 0.5 * dot(now, dot(now, now))

            sign = lax.fori_loop(0, NS_STEPS - 1, newton, sign)
            coeffs = 0.5 * (eye + sign)[0:wanted]
            mixed = jnp.concatenate([coeffs, jnp.where(narrow, 0.0, coeffs)], 0)
            basis[pair] = dot(mixed, basis[...])
            image[pair] = dot(mixed, image[...])
            square_mix = pad_rows(mixed)
            gram_ref[...] = dot_nt(dot(square_mix, gram_b), square_mix)
            cross_ref[...] = dot_nt(dot(square_mix, cross), square_mix)

        return carry

    lax.fori_loop(0, ITERS + 1, section, 0)
    out_x[...] = basis[0:wanted]
    out_p[...] = basis[wanted : 2 * wanted]
    out_r[...] = basis[third]
    out_ip[...] = image[wanted : 2 * wanted]


def hand_on(*refs):
    for source, target in zip(refs[:4], refs[4:]):
        target[...] = source[...]


def local(
    n_row, n_col,
    blocks, pattern_rows, pattern_cols, live_count, degree_scale, eigen_block, direction, cutoff,
):
    block_set = blocks[0, 0]
    slots, side, _ = block_set.shape
    wanted, docs = eigen_block.shape
    piece = docs // side
    out_rows = n_col * piece
    row_index = pattern_rows[0, 0]
    slot_id = jnp.arange(slots, dtype=jnp.int32)
    target = jnp.concatenate([row_index, jnp.arange(out_rows, dtype=jnp.int32)])
    bound = jnp.concatenate([slot_id, jnp.full((out_rows,), slots, jnp.int32)])
    before = (
        (target[:, None] == row_index[None, :])
        & (slot_id[None, :] < bound[:, None])
        & (slot_id[None, :] < live_count[0, 0])
    )
    chain = jnp.max(jnp.where(before, slot_id[None, :], -1), axis=1)
    chain = jnp.where(chain < 0, slots, chain)
    tables = jnp.concatenate([pattern_cols[0, 0], chain]).astype(jnp.int32)

    turns = ITERS + 1
    bf16, f32 = jnp.bfloat16, jnp.float32
    sem = pltpu.SemaphoreType.DMA
    vmem = pl.BlockSpec(memory_space=pltpu.VMEM)
    smem = pl.BlockSpec(memory_space=pltpu.SMEM)
    out = jax.ShapeDtypeStruct((wanted, docs), f32)
    results = pl.pallas_call(
        functools.partial(body, n_row, n_col, piece, slots, wanted),
        out_shape=(out, out, out, out),
        in_specs=[smem, smem, pl.BlockSpec(memory_space=pl.ANY), vmem, vmem, vmem],
        out_specs=(vmem, vmem, vmem, vmem),
        scratch_shapes=[
            pltpu.VMEM((slots, side, side), bf16),
            pltpu.VMEM((LANES, docs), f32),
            pltpu.VMEM((LANES, docs), f32),
            pltpu.VMEM((n_row * piece, 2 * wanted, side), bf16),
            pltpu.VMEM((slots + 1, 2 * wanted, side), f32),
            pltpu.VMEM((1, n_row * piece, 2 * wanted, side), bf16),
            pltpu.VMEM((ITERS, n_row * piece, wanted, side), bf16),
            pltpu.VMEM((1, n_col - 1, piece, 2 * wanted, side), bf16),
            pltpu.VMEM((ITERS, n_col - 1, piece, wanted, side), bf16),
            pltpu.VMEM((1, n_col - 1, piece, 2 * wanted, side), bf16),
            pltpu.VMEM((ITERS, n_col - 1, piece, wanted, side), bf16),
            pltpu.VMEM((turns, n_col, LANES // n_col, LANES), f32),
            pltpu.VMEM((turns, n_col, LANES // n_col, LANES), f32),
            pltpu.VMEM((turns, n_row, LANES // n_col, LANES), f32),
            pltpu.VMEM((turns, n_col, LANES // n_col, LANES), f32),
            pltpu.VMEM((LANES, LANES), f32),
            pltpu.VMEM((LANES, LANES), f32),
            sem,
            sem((1, n_row - 1)),
            sem((1, n_row - 1)),
            sem((ITERS, n_row - 1)),
            sem((ITERS, n_row - 1)),
            sem((1, n_col - 1)),
            sem((1, n_col - 1)),
            sem((ITERS, n_col - 1)),
            sem((ITERS, n_col - 1)),
            sem((turns, n_col - 1)),
            sem((turns, n_col - 1)),
            sem((turns, n_row - 1)),
            sem((turns, n_row - 1)),
            sem((turns, n_col - 1)),
            sem((turns, n_col - 1)),
        ],
        compiler_params=pltpu.CompilerParams(
            collective_id=0, has_side_effects=True, vmem_limit_bytes=56 * 1024 * 1024
        ),
    )(tables, cutoff, block_set, degree_scale, eigen_block, direction)
    return pl.pallas_call(
        hand_on,
        out_shape=(out, out, out, out),
        in_specs=[vmem] * 4,
        out_specs=(vmem, vmem, vmem, vmem),
    )(*results)


def solution(mesh):
    placed = (
        P("brow", "bcol", None, None, None),
        P("brow", "bcol", None),
        P("brow", "bcol", None),
        P("brow", "bcol"),
        P(("brow", "bcol")),
        P(None, ("brow", "bcol")),
        P(None, ("brow", "bcol")),
        P(),
    )
    return jax.shard_map(
        functools.partial(local, mesh.shape["brow"], mesh.shape["bcol"]),
        mesh=mesh,
        in_specs=placed,
        out_specs=(
            P(None, ("brow", "bcol")),
            P(None, ("brow", "bcol")),
            P(None, ("brow", "bcol")),
            P(None, ("brow", "bcol")),
        ),
        check_vma=False,
    )
```

profile of v0, /device:TPU:0, one launch (start us, length us, event | category | flops | bytes accessed | tf_op | source)
XLA Modules:
  0.0 113.2 jit_solution(9363123098418700434)
XLA Ops:
  1.9 0.7 pad_add_fusion
  2.7 0.8 select_reduce_fusion
  3.5 1.2 %pad_add_fusion.1.tables = s32[104]{0:T(128)} fusion(s32[64]{0:T(128)S(1)} %compare_select_fusion, s32[40]{0:T(128)} %bitcast.8), kind=kLoop, calls=%fused_computation.6 | loop fusion | flops 104 | bytes 832 | tf_op jit(solution)/shard_map/concatenate | solution.py:413
  4.7 106.7 %shard_map.111 = (f32[32,768]{1,0:T(8,128)}, f32[32,768]{1,0:T(8,128)}, f32[32,768]{1,0:T(8,128)}, f32[32,768]{1,0:T(8,128)}) custom-call(s32[104]{0:T(128)} %pad_add_fusion.1.tables, f32[1]{0:T(128)S(6)} %copy.13.cutoff, bf16[40,256,256]{2,1,0:T(8,128)(2,1)} %bitcast.5, f32[768]{0:T(1024)} %scale_ref.1, f32[32,768]{1,0:T(8,128)} %eigen_ref.1, ...), custom_call_target="tpu_custom_call" | custom-call | tf_op jit(solution)/shard_map/pallas_call | solution.py:421
  111.4 1.8 %shard_map.112 = (f32[32,768]{1,0:T(8,128)}, f32[32,768]{1,0:T(8,128)}, f32[32,768]{1,0:T(8,128)}, f32[32,768]{1,0:T(8,128)}) custom-call(f32[32,768]{1,0:T(8,128)} %get-tuple-element.8.refs_0_, f32[32,768]{1,0:T(8,128)} %get-tuple-element.9.refs_1_, f32[32,768]{1,0:T(8,128)} %get-tuple-element.10.refs_2_, f32[32,768]{1,0:T(8,128)} %get-tuple-element.11.refs_3_), custom_call_target="tpu_custom_call" | custom-call | tf_op jit(solution)/shard_map/pallas_call | solution.py:464
  (3 shorter events, 0.0 us)
where the time goes:
time: 113 us
  Pallas kernels  108 us (96%)
  other arithmetic  2.75 us (2%)
  between operations  1.95 us (2%)
    pallas_call x1, Pallas kernels, local(): pl.pallas_call(functools.partial(body, n_row, n_col, piece, slots, wanted...  107 us

commit v1 on v0

v1 whole, which is shorter than its diff:
```python
import functools

import jax
import jax.numpy as jnp
from jax import lax
from jax.experimental import pallas as pl
from jax.experimental.pallas import tpu as pltpu
from jax.sharding import PartitionSpec as P

ITERS = 2
NS_STEPS = 8
MESH = pl.DeviceIdType.MESH
LANES = 128


def halves(value):
    high = value.astype(jnp.bfloat16)
    return high, (value - high.astype(jnp.float32)).astype(jnp.bfloat16)


def split_dot(left, right, right_dim):
    rows = left.shape[0]
    left_high, left_low = halves(left)
    right_high, right_low = halves(right)

    def part(first, second):
        return lax.dot_general(
            first,
            second,
            (((1,), (right_dim,)), ((), ())),
            preferred_element_type=jnp.float32,
        )

    main = part(jnp.concatenate([left_high, left_low], 0), right_high)
    return main[:rows] + (main[rows:] + part(left_high, right_low))


def dot(left, right):
    return split_dot(left, right, 0)


def dot_nt(left, right):
    return split_dot(left, right, 1)


def grid_ids(rows):
    shape = (rows, LANES)
    return (
        lax.broadcasted_iota(jnp.int32, shape, 0),
        lax.broadcasted_iota(jnp.int32, shape, 1),
    )


def pad_rows(value, before=0):
    parts = [value, jnp.zeros((LANES - before - value.shape[0], LANES), jnp.float32)]
    if before:
        parts.insert(0, jnp.zeros((before, LANES), jnp.float32))
    return jnp.concatenate(parts, 0)


def inverse_pair(a, b, d):
    scale = 1.0 / (a * d - b * b)
    return d * scale, -(b * scale), a * scale


def inverse_four(m):
    p, q, r = inverse_pair(m[0][0], m[0][1], m[1][1])
    e = [[p * m[0][2 + c] + q * m[1][2 + c] for c in range(2)],
         [q * m[0][2 + c] + r * m[1][2 + c] for c in range(2)]]

    def schur(i, j):
        return m[2 + i][2 + j] - (m[0][2 + i] * e[0][j] + m[1][2 + i] * e[1][j])

    x, y, z = inverse_pair(schur(0, 0), schur(0, 1), schur(1, 1))
    f = [[e[i][0] * x + e[i][1] * y, e[i][0] * y + e[i][1] * z] for i in range(2)]

    def corner(i, j):
        return f[i][0] * e[j][0] + f[i][1] * e[j][1]

    off = q + corner(0, 1)
    return [
        [p + corner(0, 0), off, -f[0][0], -f[0][1]],
        [off, r + corner(1, 1), -f[1][0], -f[1][1]],
        [-f[0][0], -f[1][0], x, y],
        [-f[0][1], -f[1][1], y, z],
    ]


def inverse(matrix):
    side = matrix.shape[0]
    row_id, col_id = grid_ids(side)
    width = 4
    assert side % width == 0

    def sweep(step, now):
        first = step * width
        at_row = [row_id == first + k for k in range(width)]
        at_col = [col_id == first + k for k in range(width)]
        cols = [
            jnp.sum(jnp.where(at_col[k], now, 0.0), axis=1, keepdims=True)
            for k in range(width)
        ]
        rows = [
            jnp.sum(jnp.where(at_row[k], now, 0.0), axis=0, keepdims=True)
            for k in range(width)
        ]
        wide = [jnp.broadcast_to(col, now.shape) for col in cols]
        pivots = [
            [
                jnp.sum(jnp.where(at_row[i], wide[j], 0.0), axis=0, keepdims=True)
                for j in range(width)
            ]
            for i in range(width)
        ]
        inner = inverse_four(pivots)
        scaled_rows = [
            (inner[i][0] * rows[0] + inner[i][1] * rows[1])
            + (inner[i][2] * rows[2] + inner[i][3] * rows[3])
            for i in range(width)
        ]
        out = now - (
            (wide[0] * scaled_rows[0] + wide[1] * scaled_rows[1])
            + (wide[2] * scaled_rows[2] + wide[3] * scaled_rows[3])
        )
        for i in range(width):
            scaled_col = (wide[0] * inner[0][i] + wide[1] * inner[1][i]) + (
                wide[2] * inner[2][i] + wide[3] * inner[3][i]
            )
            out = jnp.where(at_col[i], scaled_col, out)
        for i in range(width):
            line = scaled_rows[i]
            for j in range(width):
                line = jnp.where(at_col[j][0:1], -inner[i][j], line)
            out = jnp.where(at_row[i], line, out)
        return out

    return -lax.fori_loop(0, side // width, sweep, matrix)


def extend_inverse(known, border, offset):
    side = border.shape[0]
    row_id, col_id = grid_ids(side)
    placed = (col_id == row_id + offset).astype(jnp.float32)
    edge = pad_rows(placed - dot(border, known))
    middle = inverse(dot_nt(border, edge))
    return known + dot(edge.T, pad_rows(dot(middle, edge)))


def body(
    n_row, n_col, piece, slots, wanted,
    col_table, prev_table, last_table, cutoff, blocks_hbm, scale_ref, eigen_ref, direction_ref,
    out_x, out_p, out_r, out_ip,
    blocks, basis, image, moved, work, sums, gather, part, land, kept,
    own_x, cols_x, rows_x, all_x, pair_cols, pair_rows, gram_ref, cross_ref,
    block_sem, g_send, g_recv, p_send, p_recv,
    c_send, c_recv, r_send, r_recv, a_send, a_recv, d_send, d_recv, e_send, e_recv,
):
    me_row, me_col = lax.axis_index("brow"), lax.axis_index("bcol")
    side = blocks.shape[-1]
    block_copy = pltpu.make_async_copy(blocks_hbm, blocks, block_sem)
    block_copy.start()

    def row_peer(step):
        return lax.rem(me_row + step, n_row)

    def col_peer(step):
        return lax.rem(me_col + step, n_col)

    barrier = pltpu.get_barrier_semaphore()
    for step in range(1, n_row):
        pl.semaphore_signal(
            barrier, inc=1, device_id=(row_peer(step), me_col), device_id_type=MESH
        )
    for step in range(1, n_col):
        pl.semaphore_signal(
            barrier, inc=1, device_id=(me_row, col_peer(step)), device_id_type=MESH
        )

    scale = scale_ref[...].reshape(1, piece * side)
    basis[0:wanted] = eigen_ref[...]
    basis[wanted : 2 * wanted] = direction_ref[...]
    basis[2 * wanted :] = jnp.zeros((LANES - 2 * wanted, piece * side), jnp.float32)
    image[...] = jnp.zeros(image.shape, jnp.float32)
    sums[slots] = jnp.zeros(sums.shape[1:], jnp.float32)

    pl.semaphore_wait(barrier, n_row + n_col - 2)
    row_id, col_id = grid_ids(LANES)
    eye = jnp.where((row_id == col_id) & (row_id < 3 * wanted), 1.0, 0.0)

    def remote(src, dst, send, recv, device):
        return pltpu.make_async_remote_copy(
            src_ref=src, dst_ref=dst, send_sem=send, recv_sem=recv,
            device_id=device, device_id_type=MESH,
        )

    def spot(p):
        return slice(p * side, (p + 1) * side)

    def gather_copies(phase):
        mine = pl.ds(me_row * piece, piece)
        return [
            remote(
                gather.at[phase, mine], gather.at[phase, mine],
                g_send.at[phase, step - 1], g_recv.at[phase, step - 1],
                (row_peer(step), me_col),
            )
            for step in range(1, n_row)
        ]

    def start_gather(phase, panel, first):
        for p in range(piece):
            gather[phase, me_row * piece + p] = (
                scale[:, spot(p)] * panel[first : first + wanted, spot(p)]
            ).astype(jnp.bfloat16)
        for copy in gather_copies(phase):
            copy.start()

    def finish_gather(phase):
        for copy in gather_copies(phase):
            copy.wait()

        def move(k, carry):
            work[k] = gather[phase, k]
            return carry

        lax.fori_loop(0, n_row * piece, move, 0, unroll=4)

    def multiply():
        group = 4
        assert slots % group == 0

        def some(step, carry):
            products = [
                lax.dot_general(
                    work[col_table[step * group + k]],
                    blocks[step * group + k],
                    (((1,), (1,)), ((), ())),
                    preferred_element_type=jnp.float32,
                )
                for k in range(group)
            ]
            for k in range(group):
                sums[step * group + k] = products[k] + sums[prev_table[step * group + k]]
            return carry

        lax.fori_loop(0, slots // group, some, 0, unroll=2)

    def scatter_copies(phase):
        return [
            remote(
                part.at[phase, step - 1], land.at[phase, step - 1],
                p_send.at[phase, step - 1], p_recv.at[phase, step - 1],
                (me_row, col_peer(step)),
            )
            for step in range(1, n_col)
        ]

    def fill_scatter(phase, start):
        copies = scatter_copies(phase) if start else []
        for step in range(1, n_col):
            owner = col_peer(step)
            for p in range(piece):
                part[phase, step - 1, p] = sums[last_table[owner * piece + p]].astype(
                    jnp.bfloat16
                )
            if start:
                copies[step - 1].start()
        for p in range(piece):
            kept[phase, p] = sums[last_table[me_col * piece + p]]

    def finish_scatter(phase, panel, first, target):
        for copy in scatter_copies(phase):
            copy.wait()
        for p in range(piece):
            total = kept[phase, p]
            for step in range(1, n_col):
                total = total + land[phase, step - 1, p].astype(jnp.float32)
            image[target : target + wanted, spot(p)] = (
                panel[first : first + wanted, spot(p)] - scale[:, spot(p)] * total
            )

    def swap_copies(turn, land, send, recv, along_col, source):
        me = me_col if along_col else me_row
        copies = []
        for step in range(1, n_col if along_col else n_row):
            peer = col_peer(step) if along_col else row_peer(step)
            device = (me_row, peer) if along_col else (peer, me_col)
            copies.append(
                remote(
                    source(peer), land.at[turn, me],
                    send.at[turn, step - 1], recv.at[turn, step - 1], device,
                )
            )
        return copies

    def swap(*args):
        copies = swap_copies(*args)
        for copy in copies:
            copy.start()
        for copy in copies:
            copy.wait()

    def total_of(land, turn, count):
        value = land[turn, 0]
        for k in range(1, count):
            value = value + land[turn, k]
        return value

    def add_up(turn, value):
        height = LANES // n_col
        for k in range(n_col):
            own_x[turn, k] = value[k * height : (k + 1) * height]
        cols_x[turn, me_col] = own_x[turn, me_col]
        swap(turn, cols_x, c_send, c_recv, True, lambda peer: own_x.at[turn, peer])
        rows_x[turn, me_row] = total_of(cols_x, turn, n_col)
        swap(turn, rows_x, r_send, r_recv, False, lambda peer: rows_x.at[turn, me_row])
        all_x[turn, me_col] = total_of(rows_x, turn, n_row)
        swap(turn, all_x, a_send, a_recv, True, lambda peer: all_x.at[turn, me_col])
        return jnp.concatenate([all_x[turn, k] for k in range(n_col)], 0)

    pair = slice(0, 2 * wanted)
    third = slice(2 * wanted, 3 * wanted)
    narrow = grid_ids(wanted)[1] < wanted
    half = grid_ids(wanted)[1] < 2 * wanted

    start_gather(0, basis, 0)
    block_copy.wait()
    finish_gather(0)
    start_gather(1, basis, wanted)
    multiply()
    fill_scatter(0, True)
    finish_gather(1)
    multiply()
    fill_scatter(1, False)
    finish_scatter(0, basis, 0, 0)
    moved[0:wanted] = basis[0:wanted] - image[0:wanted]
    moved[wanted:] = jnp.zeros((LANES - wanted, piece * side), jnp.float32)
    start_gather(2, moved, 0)
    for copy in scatter_copies(1):
        copy.start()
    finish_scatter(1, basis, wanted, wanted)

    def pair_swap():
        return swap_copies(
            0, pair_cols, d_send, d_recv, True, lambda peer: pair_cols.at[0, me_col]
        )

    both = jnp.concatenate([basis[pair], image[pair]], 0)
    pair_cols[0, me_col] = dot_nt(basis[pair], both)
    for copy in pair_swap():
        copy.start()

    def find_residual():
        gram_inv = pad_rows(inverse(jnp.where(narrow, gram_ref[0:wanted], 0.0)))
        rayleigh_t = jnp.where(narrow, cross_ref[...].T[0:wanted], 0.0)
        quotient_t = dot(rayleigh_t, gram_inv)
        basis[third] = image[0:wanted] - dot(quotient_t, basis[...])
        return gram_inv, quotient_t

    def iteration(turn, carry):
        finish_gather(turn + 2)
        multiply()
        fill_scatter(turn + 2, True)

        @pl.when(turn == 0)
        def _():
            for copy in pair_swap():
                copy.wait()
            pair_rows[0, me_row] = total_of(pair_cols, 0, n_col)
            swap(0, pair_rows, e_send, e_recv, False, lambda peer: pair_rows.at[0, me_row])
            grams = pad_rows(total_of(pair_rows, 0, n_row))
            gram_ref[...] = jnp.where(col_id < 2 * wanted, grams, 0.0)
            cross_ref[...] = pad_rows(grams.T[2 * wanted :]).T

        gram_inv, quotient_t = find_residual()
        gram_pair = gram_ref[...]
        cross_pair = cross_ref[...]
        pair_inv = extend_inverse(
            gram_inv, jnp.where(half, gram_pair[wanted : 2 * wanted], 0.0), wanted
        )
        turned = basis[third] + dot(quotient_t, moved[...])
        finish_scatter(turn + 2, moved, 0, 2 * wanted)
        image[third] = turned - image[third]
        everything = jnp.concatenate([basis[...], image[...]], 0)
        by_residual = dot_nt(basis[third], everything)
        border = add_up(
            turn,
            pad_rows(
                jnp.concatenate(
                    [
                        by_residual[:, :LANES],
                        by_residual[:, LANES:],
                        dot_nt(image[third], basis[...]),
                    ],
                    0,
                )
            ),
        )

        def around(rows, cols):
            low = pad_rows(rows, 2 * wanted)
            right = pad_rows(cols, 2 * wanted).T
            return low + jnp.where(row_id < 2 * wanted, right, 0.0)

        full_inv = extend_inverse(pair_inv, border[0:wanted], 2 * wanted)
        gram_b = gram_pair + around(border[0:wanted], border[0:wanted])
        cross = cross_pair + around(border[wanted : 2 * wanted], border[third])
        gram_a = 0.5 * (cross + cross.T)
        shifted = cutoff[0] * eye - dot(gram_a, full_inv)
        square = dot(shifted, shifted)
        trace = jnp.sum(
            jnp.sum(jnp.where(row_id == col_id, square, 0.0), axis=1, keepdims=True),
            axis=0,
            keepdims=True,
        )
        norm = 1.0 / jnp.sqrt(trace + 1e-06)
        sign = (1.5 * norm) * shifted - (0.5 * norm) * dot(
            shifted * norm, square * norm
        )

        def newton(_, now):
            return 1.5 * now - 0.5 * dot(now, dot(now, now))

        sign = lax.fori_loop(0, NS_STEPS - 1, newton, sign)
        coeffs = 0.5 * (eye + sign)[0:wanted]
        mixed = jnp.concatenate([coeffs, jnp.where(narrow, 0.0, coeffs)], 0)
        basis[pair] = dot(mixed, basis[...])
        image[pair] = dot(mixed, image[...])

        @pl.when(turn + 1 < ITERS)
        def _():
            moved[0:wanted] = basis[0:wanted] - image[0:wanted]
            start_gather(turn + 3, moved, 0)

        square_mix = pad_rows(mixed)
        gram_ref[...] = dot_nt(dot(square_mix, gram_b), square_mix)
        cross_ref[...] = dot_nt(dot(square_mix, cross), square_mix)
        return carry

    lax.fori_loop(0, ITERS, iteration, 0)
    find_residual()
    out_x[...] = basis[0:wanted]
    out_p[...] = basis[wanted : 2 * wanted]
    out_r[...] = basis[third]
    out_ip[...] = image[wanted : 2 * wanted]


def hand_on(*refs):
    for source, target in zip(refs[:4], refs[4:]):
        target[...] = source[...]


def local(
    n_row, n_col,
    blocks, pattern_rows, pattern_cols, live_count, degree_scale, eigen_block, direction, cutoff,
):
    block_set = blocks[0, 0]
    slots, side, _ = block_set.shape
    wanted, docs = eigen_block.shape
    piece = docs // side
    out_rows = n_col * piece
    row_index = pattern_rows[0, 0]
    slot_id = jnp.arange(slots, dtype=jnp.int32)

    def latest(rows, bound):
        fits = (
            (rows[:, None] == row_index[None, :])
            & (slot_id[None, :] < bound[:, None])
            & (slot_id[None, :] < live_count[0, 0])
        )
        found = jnp.max(jnp.where(fits, slot_id[None, :], -1), axis=1)
        return jnp.where(found < 0, slots, found).astype(jnp.int32)

    previous = latest(row_index, slot_id)
    last = latest(
        jnp.arange(out_rows, dtype=jnp.int32), jnp.full((out_rows,), slots, jnp.int32)
    )

    phases = ITERS + 2
    height = LANES // n_col
    bf16, f32 = jnp.bfloat16, jnp.float32
    sem = pltpu.SemaphoreType.DMA
    vmem = pl.BlockSpec(memory_space=pltpu.VMEM)
    smem = pl.BlockSpec(memory_space=pltpu.SMEM)
    out = jax.ShapeDtypeStruct((wanted, docs), f32)
    results = pl.pallas_call(
        functools.partial(body, n_row, n_col, piece, slots, wanted),
        out_shape=(out, out, out, out),
        in_specs=[smem, smem, smem, smem, pl.BlockSpec(memory_space=pl.ANY), vmem, vmem, vmem],
        out_specs=(vmem, vmem, vmem, vmem),
        scratch_shapes=[
            pltpu.VMEM((slots, side, side), bf16),
            pltpu.VMEM((LANES, docs), f32),
            pltpu.VMEM((LANES, docs), f32),
            pltpu.VMEM((LANES, docs), f32),
            pltpu.VMEM((n_row * piece, wanted, side), bf16),
            pltpu.VMEM((slots + 1, wanted, side), f32),
            pltpu.VMEM((phases, n_row * piece, wanted, side), bf16),
            pltpu.VMEM((phases, n_col - 1, piece, wanted, side), bf16),
            pltpu.VMEM((phases, n_col - 1, piece, wanted, side), bf16),
            pltpu.VMEM((phases, piece, wanted, side), f32),
            pltpu.VMEM((ITERS, n_col, height, LANES), f32),
            pltpu.VMEM((ITERS, n_col, height, LANES), f32),
            pltpu.VMEM((ITERS, n_row, height, LANES), f32),
            pltpu.VMEM((ITERS, n_col, height, LANES), f32),
            pltpu.VMEM((1, n_col, 2 * wanted, LANES), f32),
            pltpu.VMEM((1, n_row, 2 * wanted, LANES), f32),
            pltpu.VMEM((LANES, LANES), f32),
            pltpu.VMEM((LANES, LANES), f32),
            sem,
            sem((phases, n_row - 1)),
            sem((phases, n_row - 1)),
            sem((phases, n_col - 1)),
            sem((phases, n_col - 1)),
            sem((ITERS, n_col - 1)),
            sem((ITERS, n_col - 1)),
            sem((ITERS, n_row - 1)),
            sem((ITERS, n_row - 1)),
            sem((ITERS, n_col - 1)),
            sem((ITERS, n_col - 1)),
            sem((1, n_col - 1)),
            sem((1, n_col - 1)),
            sem((1, n_row - 1)),
            sem((1, n_row - 1)),
        ],
        compiler_params=pltpu.CompilerParams(
            collective_id=0, has_side_effects=True, vmem_limit_bytes=56 * 1024 * 1024
        ),
    )(pattern_cols[0, 0], previous, last, cutoff, block_set, degree_scale, eigen_block, direction)
    return pl.pallas_call(
        hand_on,
        out_shape=(out, out, out, out),
        in_specs=[vmem] * 4,
        out_specs=(vmem, vmem, vmem, vmem),
    )(*results)


def solution(mesh):
    placed = (
        P("brow", "bcol", None, None, None),
        P("brow", "bcol", None),
        P("brow", "bcol", None),
        P("brow", "bcol"),
        P(("brow", "bcol")),
        P(None, ("brow", "bcol")),
        P(None, ("brow", "bcol")),
        P(),
    )
    return jax.shard_map(
        functools.partial(local, mesh.shape["brow"], mesh.shape["bcol"]),
        mesh=mesh,
        in_specs=placed,
        out_specs=(
            P(None, ("brow", "bcol")),
            P(None, ("brow", "bcol")),
            P(None, ("brow", "bcol")),
            P(None, ("brow", "bcol")),
        ),
        check_vma=False,
    )
```

time: 113 us -> 95.8 us (0.85)
  Pallas kernels: 108 us -> 91 us
    pallas_call x1, Pallas kernels: 107 us -> 89.3 us  [local(): pl.pallas_call(functools.partial(body, n_row, n_col, piece, slots, wanted...]
    concatenate x2 -> x0, other arithmetic: 1.97 us -> none  [the longest x1 1.24 us: local(): tables = jnp.concatenate([pattern_cols[0, 0], chain]).astype(jnp.int32)]
where the time goes in v1:
time: 95.8 us; the launch traced here: 95.7 us
  Pallas kernels  91 us (95%)
  other arithmetic  2.73 us (3%)
  between operations  1.94 us (2%)
    pallas_call x1, Pallas kernels, local(): pl.pallas_call(functools.partial(body, n_row, n_col, piece, slots, wanted...  89.3 us

profile of v1, /device:TPU:0, one launch (start us, length us, event | category | flops | bytes accessed | tf_op | source)
XLA Modules:
  0.0 95.7 jit_solution(6272094085639932035)
XLA Ops:
  1.9 0.8 select_reduce_fusion.1
  2.7 0.9 select_reduce_fusion
  3.6 0.5 compare_select_fusion.1.prev_table
  4.2 0.5 compare_select_fusion.last_table
  4.7 89.3 %shard_map.111 = (f32[32,768]{1,0:T(8,128)}, f32[32,768]{1,0:T(8,128)}, f32[32,768]{1,0:T(8,128)}, f32[32,768]{1,0:T(8,128)}) custom-call(s32[40]{0:T(128)} %bitcast.8, s32[40]{0:T(128)} %compare_select_fusion.1.prev_table, s32[24]{0:T(128)} %compare_select_fusion.last_table, f32[1]{0:T(128)S(6)} %copy.13.cutoff, bf16[40,256,256]{2,1,0:T(8,128)(2,1)} %bitcast.5, ...), custom_call_target="tpu_custom_call" | custom-call | tf_op jit(solution)/shard_map/pallas_call | solution.py:486
  93.9 1.8 %shard_map.112 = (f32[32,768]{1,0:T(8,128)}, f32[32,768]{1,0:T(8,128)}, f32[32,768]{1,0:T(8,128)}, f32[32,768]{1,0:T(8,128)}) custom-call(f32[32,768]{1,0:T(8,128)} %get-tuple-element.8.refs_0_, f32[32,768]{1,0:T(8,128)} %get-tuple-element.9.refs_1_, f32[32,768]{1,0:T(8,128)} %get-tuple-element.10.refs_2_, f32[32,768]{1,0:T(8,128)} %get-tuple-element.11.refs_3_), custom_call_target="tpu_custom_call" | custom-call | tf_op jit(solution)/shard_map/pallas_call | solution.py:530
  (1 shorter events, 0.0 us)
